TPU v7x, 256 devices: a whole 4x4x8 slice. The times are simulated.
256 devices in a mesh: ctx: 64 (over z, x, core), head: 4 (over y).
Axes of the slice: x: 4, y: 4, z: 8, core: 2. Of those that a mesh axis runs over, the one named last changes fastest.
Arguments:
- activations: bfloat16 [8192, 8192], P('ctx', 'head'), may hold values from -6 to 6
- adapter_down: bfloat16 [8192, 768], P('head'), may hold values from -0.0625 to 0.0625
- adapter_ids: int32 [8192, 2], P('ctx'), may hold values from 0 to 7, all different within a row
- adapter_weight: float32 [8192, 2], P('ctx'), may hold values from 0.05 to 0.95, as said below
- query_base: bfloat16 [8192, 8192], P('ctx', 'head'), may hold values from -110 to 110
- key_base: bfloat16 [8192, 1024], P('ctx', 'head'), may hold values from -6 to 6
- value_base: bfloat16 [8192, 1024], P('ctx', 'head'), may hold values from -6 to 6
- up_query: bfloat16 [256, 8192], P(None, 'head'), may hold values from -1 to 1
- up_key: bfloat16 [256, 1024], P(None, 'head'), may hold values from -1 to 1
- up_value: bfloat16 [256, 1024], P(None, 'head'), may hold values from -1 to 1
Outputs:
- attended: bfloat16 [8192, 8192], P('ctx', 'head')
Inputs may be any that keep to these rules, and one draw needn't show every extreme that they name: `adapter_weight`: each row holds two weights that sum to one, the first the larger.
All inputs are finite; a program needn't handle non-finite values.
Results may differ from a plain program's by a relative error of at most 0.029.
Values may be sent and summed in bfloat16 or wider, within the bound.
No kernel may reach another device: no remote copies, remote signals or barrier semaphores. Data moves between devices by JAX's collectives and lax.ppermute only.
A program may use at most 64 MiB of HBM per device.

v0:
```python
import functools
import math

import jax
import jax.numpy as jnp
from jax import lax
from jax.experimental import pallas as pl
from jax.experimental.pallas import tpu as pltpu
from jax.sharding import PartitionSpec as P

HD = 128
ADAPTERS = 8
RANK = 32
SPAN = ADAPTERS * RANK
ROWS = 128
GROUP = 8
ZS, XS, YS = 8, 4, 4
BLOCK = 2 * ROWS
SLAB = XS * BLOCK
SIDE = GROUP * ROWS

rope_base = 500000.0
floor_value = -1e30
FACTOR = math.log2(math.e) / math.sqrt(HD)
ROOM = 2.0**60
VMEM_LIMIT = 40 * 1024 * 1024


def device(z, x, core, y):
    return (((z % ZS) * XS + x % XS) * 2 + core) * YS + y


def send(array, move):
    pairs = []
    for z in range(ZS):
        for x in range(XS):
            for core in range(2):
                for y in range(YS):
                    pairs.append((device(z, x, core, y), device(*move(z, x, core, y))))
    return lax.ppermute(array, ("ctx", "head"), pairs)


def swap_cores(array):
    return send(array, lambda z, x, core, y: (z, x, 1 - core, y))


def turn(raw, cosine, sine):
    return raw * cosine + pltpu.roll(raw, HD // 2, 1) * sine


def low_kernel(act_hbm, down_hbm, low_ref, sent_ref, act_ref, down_ref, act_sem, down_sem):
    pieces = act_sem.shape[0]
    depth = act_ref.shape[1] // pieces
    copies = []
    for k in range(pieces):
        span = slice(k * depth, (k + 1) * depth)
        copies.append(
            (
                pltpu.make_async_copy(act_hbm.at[:, span], act_ref.at[:, span], act_sem.at[k]),
                pltpu.make_async_copy(down_hbm.at[span], down_ref.at[span], down_sem.at[k]),
            )
        )
        for copy in copies[-1]:
            copy.start()
    total = None
    for k in range(pieces):
        span = slice(k * depth, (k + 1) * depth)
        for copy in copies[k]:
            copy.wait()
        part = jnp.dot(act_ref[:, span], down_ref[span], preferred_element_type=jnp.float32)
        total = part if total is None else total + part
    low_ref[...] = total
    sent_ref[...] = total.astype(jnp.bfloat16)


def low_product(activations, adapter_down):
    rows, columns = activations.shape[0], adapter_down.shape[1]
    pieces = 4
    return pl.pallas_call(
        low_kernel,
        in_specs=[pl.BlockSpec(memory_space=pltpu.HBM)] * 2,
        out_specs=(whole(), whole()),
        out_shape=(
            jax.ShapeDtypeStruct((rows, columns), jnp.float32),
            jax.ShapeDtypeStruct((rows, columns), jnp.bfloat16),
        ),
        scratch_shapes=[
            pltpu.VMEM(activations.shape, activations.dtype),
            pltpu.VMEM(adapter_down.shape, adapter_down.dtype),
            pltpu.SemaphoreType.DMA((pieces,)),
            pltpu.SemaphoreType.DMA((pieces,)),
        ],
        compiler_params=pltpu.CompilerParams(vmem_limit_bytes=56 * 1024 * 1024),
        cost_estimate=pl.CostEstimate(flops=1 << 29, bytes_accessed=4 << 20, transcendentals=0),
    )(activations, adapter_down)


def add_kernel(low_ref, got_ref, sum_ref, sent_ref):
    total = low_ref[...] + got_ref[...].astype(jnp.float32)
    sum_ref[...] = total
    sent_ref[...] = total.astype(jnp.bfloat16)


def gated(low, more, coef):
    return ((low + more.astype(jnp.float32)) * coef).astype(jnp.bfloat16)


def kv_kernel(group_ref, low_ref, more_ref, coef_ref, upk_ref, upv_ref, kb_ref, vb_ref, cos_ref, sin_ref, mine_ref, other_ref, gq_ref):
    group = group_ref[0]
    coef = coef_ref[...]
    gq_ref[...], gk, gv = [
        gated(low_ref[:, p * SPAN : (p + 1) * SPAN], more_ref[:, p * SPAN : (p + 1) * SPAN], coef) for p in range(3)
    ]
    key_raw = kb_ref[...].astype(jnp.float32) + jnp.dot(gk, upk_ref[...], preferred_element_type=jnp.float32)
    value = vb_ref[...].astype(jnp.float32) + jnp.dot(gv, upv_ref[...], preferred_element_type=jnp.float32)
    cosine, sine = cos_ref[...], sin_ref[...]
    keys = [turn(key_raw[:, h * HD : (h + 1) * HD], cosine, sine) for h in range(2)]
    values = [value[:, h * HD : (h + 1) * HD] for h in range(2)]
    first = group == 0
    mine_ref[:, :HD] = jnp.where(first, keys[0], keys[1]).astype(jnp.bfloat16)
    mine_ref[:, HD:] = jnp.where(first, values[0], values[1]).astype(jnp.bfloat16)
    other_ref[:, :HD] = jnp.where(first, keys[1], keys[0]).astype(jnp.bfloat16)
    other_ref[:, HD:] = jnp.where(first, values[1], values[0]).astype(jnp.bfloat16)


def q_kernel(group_ref, gq_ref, upq_ref, qb_ref, cos_ref, sin_ref, mine_ref, *other_refs):
    own = group_ref[0]
    cosine, sine = cos_ref[...], sin_ref[...]
    gq = gq_ref[...]
    start = (1 - own) * GROUP
    for target in (*other_refs, mine_ref):
        heads = target.shape[1] // HD
        if target is mine_ref:
            start = own * GROUP
        for j in range(heads):
            cols = pl.ds(pl.multiple_of((start + j) * HD, HD), HD)
            raw = qb_ref[:, cols].astype(jnp.float32) + jnp.dot(
                gq, upq_ref[:, cols], preferred_element_type=jnp.float32
            )
            target[:, j * HD : (j + 1) * HD] = turn(raw, cosine, sine).astype(jnp.bfloat16)
        start = start + heads


def join_kernel(*refs):
    *parts, out_ref = refs
    start = 0
    for part in parts:
        out_ref[start : start + part.shape[0]] = part[...]
        start += part.shape[0]


def touch_kernel(seen_ref, in_ref, out_ref):
    out_ref[...] = in_ref[...]


def queries(refs):
    tiles = [ref[:, g * HD : (g + 1) * HD] for ref in refs for g in range(ref.shape[1] // HD)]
    return jnp.concatenate(tiles, axis=0)


def scores_of(keys, query):
    return lax.dot_general(keys, query, (((1,), (1,)), ((), ())), preferred_element_type=jnp.float32)


def weighted(values, weights):
    return lax.dot_general(values, weights, (((0,), (0,)), ((), ())), preferred_element_type=jnp.float32)


def careful(q_sides, kv_refs, states, spare, bases=None):
    gap = lax.broadcasted_iota(jnp.int32, (ROWS, HD), 1) - lax.broadcasted_iota(jnp.int32, (ROWS, HD), 0)
    q_ref, kv_ref = spare
    start = 0
    for ref in kv_refs:
        kv_ref[start : start + ref.shape[0]] = ref[...]
        start += ref.shape[0]
    for q_refs, (top_ref, total_ref, acc_ref) in zip(q_sides, states):
        start = 0
        for ref in q_refs:
            q_ref[:, start : start + ref.shape[1]] = ref[...]
            start += ref.shape[1]

        def body(i, carry, top_ref=top_ref, total_ref=total_ref, acc_ref=acc_ref):
            j, g = i // GROUP, i % GROUP
            rows = pl.ds(pl.multiple_of(j * ROWS, ROWS), ROWS)
            cols = pl.ds(pl.multiple_of(g * HD, HD), HD)
            scores = scores_of(kv_ref[rows, :HD], q_ref[:, cols])
            if bases is not None:
                scores = jnp.where(gap >= bases[j] - bases[SLAB // ROWS], scores, floor_value)
            old = top_ref[:, cols]
            top = jnp.maximum(old, jnp.max(scores, axis=0, keepdims=True) * FACTOR)
            expo = jnp.exp2(scores * FACTOR - top[:1])
            shrink = jnp.exp2(old - top)
            top_ref[:, cols] = top
            total_ref[:, cols] = total_ref[:, cols] * shrink + jnp.sum(expo.reshape(ROWS // 8, 8, HD), axis=0)
            acc_ref[:, cols] = acc_ref[:, cols] * shrink[:1] + weighted(kv_ref[rows, HD:], expo.astype(jnp.bfloat16))
            return carry

        lax.fori_loop(0, SLAB // ROWS * GROUP, body, 0)


def first_kernel(diagonal, base_ref, *refs):
    *q_refs, a_ref, b_ref, top_ref, total_ref, acc_ref, spare_q, spare_kv = refs
    kv = jnp.concatenate([a_ref[...], b_ref[...]], axis=0)
    scores = scores_of(kv[:, :HD], queries(q_refs))
    gap = lax.broadcasted_iota(jnp.int32, (ROWS, HD), 1) - lax.broadcasted_iota(jnp.int32, (ROWS, HD), 0)
    lines = [scores[j * ROWS : (j + 1) * ROWS] for j in range(SLAB // ROWS)]
    seen = jnp.concatenate([gap >= 0] * GROUP, axis=1)
    lines[diagonal] = jnp.where(seen, lines[diagonal], floor_value)
    top = jnp.max(lines[diagonal], axis=0, keepdims=True) * FACTOR
    top = jnp.broadcast_to(top, (8, SIDE))
    parts = []
    for j, line in enumerate(lines):
        hidden = jnp.where(base_ref[j] > base_ref[SLAB // ROWS], -floor_value, 0.0)
        parts.append(jnp.exp2(line.reshape(ROWS // 8, 8, SIDE) * FACTOR - (top + hidden)[None]))
    expo = jnp.concatenate(parts, axis=0)
    total = jnp.sum(expo, axis=0)
    top_ref[...] = top
    total_ref[...] = total
    acc_ref[...] = weighted(kv[:, HD:], expo.astype(jnp.bfloat16).reshape(SLAB, SIDE))

    @pl.when(jnp.logical_not(jnp.max(total) <= ROOM))
    def _():
        total_ref[...] = jnp.zeros_like(total_ref)
        acc_ref[...] = jnp.zeros_like(acc_ref)
        careful([q_refs], (a_ref, b_ref), [(top_ref, total_ref, acc_ref)], (spare_q, spare_kv), base_ref)


def part_of(query, kv, top):
    keys, cols = kv.shape[0], query.shape[0]
    scores = scores_of(kv[:, :HD], query).reshape(keys // 8, 8, cols)
    expo = jnp.exp2(scores * FACTOR - top[None])
    total = jnp.sum(expo, axis=0)
    acc = weighted(kv[:, HD:], expo.astype(jnp.bfloat16).reshape(keys, cols))
    return total, acc, jnp.max(total) <= ROOM


def next_kernel(flag_ref, *refs):
    q_refs, kv_ref, ins, outs, spare, part_ref = refs[:3], refs[3], refs[4:10], refs[10:16], refs[16:18], refs[18]

    @pl.when(flag_ref[0] == 0)
    def _():
        for ref, given in zip(outs, ins):
            ref[...] = given[...]

    @pl.when(flag_ref[0] != 0)
    def _():
        top = jnp.concatenate([ins[0][...], ins[3][...]], axis=1)
        total, part_ref[...], room = part_of(queries(q_refs), kv_ref[...], top)

        @pl.when(room)
        def _():
            for side in range(2):
                cols = slice(side * SIDE, (side + 1) * SIDE)
                outs[3 * side][...] = ins[3 * side][...]
                outs[3 * side + 1][...] = ins[3 * side + 1][...] + total[:, cols]
                outs[3 * side + 2][...] = ins[3 * side + 2][...] + part_ref[:, cols]

        @pl.when(jnp.logical_not(room))
        def _():
            for ref, given in zip(outs, ins):
                ref[...] = given[...]
            careful([q_refs[:1], q_refs[1:]], (kv_ref,), [outs[:3], outs[3:]], spare)


def loop_kernel(flag_ref, *refs):
    q_refs, kv_ref, ins, outs, spare = refs[:3], refs[3], refs[4:10], refs[10:16], refs[16:18]
    sides_q, tops, totals, accs = refs[18:]

    @pl.when(flag_ref[0] == 0)
    def _():
        for ref, given in zip(outs, ins):
            ref[...] = given[...]

    @pl.when(flag_ref[0] != 0)
    def _():
        sides_q[0] = q_refs[0][...]
        sides_q[1, :, : SIDE // 2] = q_refs[1][...]
        sides_q[1, :, SIDE // 2 :] = q_refs[2][...]
        for side in range(2):
            tops[side] = ins[3 * side][...]

        def body(side, carry):
            totals[side], accs[side], unused = part_of(queries([sides_q.at[side]]), kv_ref[...], tops[side])
            return carry

        lax.fori_loop(0, 2, body, 0)
        room = jnp.max(totals[...]) <= ROOM

        @pl.when(room)
        def _():
            for side in range(2):
                outs[3 * side][...] = ins[3 * side][...]
                outs[3 * side + 1][...] = ins[3 * side + 1][...] + totals[side]
                outs[3 * side + 2][...] = ins[3 * side + 2][...] + accs[side]

        @pl.when(jnp.logical_not(room))
        def _():
            for ref, given in zip(outs, ins):
                ref[...] = given[...]
            careful([q_refs[:1], q_refs[1:]], (kv_ref,), [outs[:3], outs[3:]], spare)


def last_kernel(flag_ref, *refs):
    *q_refs, a_ref, b_ref, top_ref, total_ref, acc_ref, out_ref, spare_q, spare_kv, last_top, last_total, last_acc = refs
    last_total[...] = total_ref[...]
    last_acc[...] = acc_ref[...]

    @pl.when(flag_ref[0] != 0)
    def _():
        kv = jnp.concatenate([a_ref[...], b_ref[...]], axis=0)
        total, acc, room = part_of(queries(q_refs), kv, top_ref[...])
        last_total[...] = total_ref[...] + total
        last_acc[...] = acc_ref[...] + acc

        @pl.when(jnp.logical_not(room))
        def _():
            last_top[...] = top_ref[...]
            last_total[...] = total_ref[...]
            last_acc[...] = acc_ref[...]
            careful([q_refs], (a_ref, b_ref), [(last_top, last_total, last_acc)], (spare_q, spare_kv))

    scale = 1.0 / jnp.sum(last_total[...], axis=0, keepdims=True)
    for g in range(GROUP):
        cols = slice(g * HD, (g + 1) * HD)
        out_ref[:, cols] = (last_acc[:, cols] * scale[:, cols]).T.astype(jnp.bfloat16)


def whole():
    return pl.BlockSpec(memory_space=pltpu.VMEM)


def call(kernel, n_in, outs, n_scalar=1, aliases=None, scratch=()):
    return pl.pallas_call(
        kernel,
        out_shape=outs,
        in_specs=[pl.BlockSpec(memory_space=pltpu.SMEM)] * n_scalar + [whole()] * n_in,
        out_specs=tuple(whole() for _ in outs),
        input_output_aliases=aliases or {},
        scratch_shapes=list(scratch),
        compiler_params=pltpu.CompilerParams(vmem_limit_bytes=VMEM_LIMIT),
        cost_estimate=pl.CostEstimate(flops=1 << 34, bytes_accessed=1 << 26, transcendentals=0),
    )


def after(array, *others):
    return lax.optimization_barrier((array,) + others)


def on_device(activations, adapter_down, adapter_ids, adapter_weight, query_base, key_base, value_base, up_query, up_key, up_value):
    ctx = lax.axis_index("ctx").astype(jnp.int32)
    z, x, core = ctx // (2 * XS), (ctx // 2) % XS, ctx % 2
    group = ((x + 1) // 2) % 2
    groups = group.reshape(1)
    f32, b16 = jnp.float32, jnp.bfloat16
    shape = jax.ShapeDtypeStruct

    low, sent = low_product(activations, adapter_down)

    def pair_up(array, step):
        return send(array, lambda z, x, c, y: (z, x, c, y ^ (1 if c == step else 3)))

    one = pair_up(sent, 0)

    labels = jnp.arange(SPAN, dtype=jnp.int32) // RANK
    coef = jnp.zeros((ROWS, SPAN), f32)
    for j in range(adapter_ids.shape[1]):
        coef = coef + jnp.where(adapter_ids[:, j : j + 1] == labels[None, :], adapter_weight[:, j : j + 1], 0.0)
    positions = (ctx * ROWS + jnp.arange(ROWS, dtype=jnp.int32)).astype(f32)
    inverse = jnp.exp(jnp.arange(HD // 2, dtype=f32) * (-2.0 * math.log(rope_base) / HD))
    angles = positions[:, None] * jnp.concatenate([inverse, inverse])[None, :]
    cosine = jnp.cos(angles)
    sign = jnp.where(jnp.arange(HD) < HD // 2, -1.0, 1.0).astype(f32)
    sine = jnp.sin(angles) * sign[None, :]
    low = call(join_kernel, 1, (shape(low.shape, f32),), 0)(low)[0]
    one, low, coef, cosine, sine = after(one, low, coef, cosine, sine)
    low, sent = call(add_kernel, 2, (shape(low.shape, f32), shape(low.shape, b16)), 0)(low, one)
    two = pair_up(sent, 1)

    kv_shape = shape((ROWS, 2 * HD), b16)
    kv, kv_other, gated_query = call(kv_kernel, 9, (kv_shape, kv_shape, shape((ROWS, SPAN), b16)))(
        groups, low, two, coef, up_key, up_value, key_base, value_base, cosine, sine
    )

    def neighbour(array):
        return send(array, lambda z, x, c, y: (z, x ^ 1, c, y))

    blocks_x = [
        neighbour(kv_other),
        send(kv, lambda z, x, c, y: (z, x ^ 3, c, y)),
        send(kv_other, lambda z, x, c, y: (z, x ^ 2, c, y)),
    ]
    side_shape = shape((ROWS, GROUP * HD), b16)
    piece_shape = shape((ROWS, GROUP * HD // 2), b16)
    q_own, *q_other = call(q_kernel, 5, (side_shape, piece_shape, piece_shape))(
        groups, gated_query, up_query, query_base, cosine, sine
    )
    *blocks_x, q_own, q_first, q_second = after(*blocks_x, q_own, *q_other)

    def join(*parts):
        rows = sum(part.shape[0] for part in parts)
        return call(join_kernel, len(parts), (shape((rows, 2 * HD), b16),), 0)(*parts)[0]

    moving_a = join(kv, *blocks_x)
    q_rest = [neighbour(q_first), neighbour(q_second)]

    def ring(array):
        return send(array, lambda z, x, c, y: (z + (1 if c == 0 else -1), x, c, y))

    arriving_a = ring(moving_a)
    moving_b = swap_cores(moving_a)
    moving_b, q_rest[0] = after(moving_b, q_rest[0])
    arriving_b = ring(moving_b)

    blocks = (jnp.stack([x, x ^ 1, x ^ 3, x ^ 2]) - x) * BLOCK
    keys_at = jnp.concatenate([blocks + core * ROWS, blocks + (1 - core) * ROWS])

    def bases(start):
        return jnp.concatenate([keys_at, start.reshape(1)]).astype(jnp.int32)

    spare = [pltpu.VMEM((ROWS, SIDE), b16), pltpu.VMEM((SLAB, 2 * HD), b16)]
    state_shape = (shape((8, SIDE), f32), shape((8, SIDE), f32), shape((HD, SIDE), f32))
    state = [
        *call(functools.partial(first_kernel, 0), 3, state_shape, scratch=spare)(bases(core * ROWS), q_own, moving_a, moving_b),
    ]
    state += call(functools.partial(first_kernel, 1), 4, state_shape, scratch=spare)(
        bases(((x ^ 1) - x) * BLOCK + core * ROWS), *q_rest, moving_a, moving_b
    )

    def attend(kernel, scratch, flag, kv, state):
        aliases = {5 + k: k for k in range(6)}
        return call(kernel, 10, state_shape * 2, 1, aliases, spare + scratch)(
            flag.astype(jnp.int32).reshape(1), q_own, *q_rest, kv, *state
        )

    near = functools.partial(attend, next_kernel, [pltpu.VMEM((HD, 2 * SIDE), f32)])
    sides = [((2, ROWS, SIDE), b16), ((2, 8, SIDE), f32), ((2, 8, SIDE), f32), ((2, HD, SIDE), f32)]
    away = functools.partial(attend, loop_kernel, [pltpu.VMEM(*side) for side in sides])

    def take(arriving, state, on):
        arrived, *state = after(arriving, *state)
        if not on:
            return arrived, None, state
        arriving = ring(arrived)
        top = call(touch_kernel, 2, state_shape[:1], 0, {1: 0})(arrived, state[0])[0]
        return arrived, arriving, [top, *state[1:]]

    next_a, arriving_a, state = take(arriving_a, state, True)
    for step in range(1, 4):
        below, wrapped = z >= step, z + step >= ZS
        moving_b, arriving_b, state = take(arriving_b, state, True)
        moving = join(next_a, moving_b)
        swapped = swap_cores(moving)
        state = near(jnp.where(core == 0, below, wrapped), moving, state)
        next_a, arriving_a, state = take(arriving_a, state, step < 3)
        state = away(jnp.where(core == 0, wrapped, below), swapped, state)
    moving_a = next_a
    moving_b, *state = after(arriving_b, *state)
    flag = (z >= ZS // 2).astype(jnp.int32).reshape(1)

    def finish(query, state):
        scratch = spare + [pltpu.VMEM((8, SIDE), f32)] * 2 + [pltpu.VMEM((HD, SIDE), f32)]
        return call(last_kernel, len(query) + 5, (side_shape,), scratch=scratch)(
            flag, *query, moving_a, moving_b, *state
        )[0]

    back = neighbour(finish(q_rest, state[3:]))
    own = finish([q_own], state[:3])
    return jnp.concatenate([jnp.where(group == 0, own, back), jnp.where(group == 0, back, own)], axis=1)


def solution(mesh):
    in_specs = (
        P("ctx", "head"),
        P("head", None),
        P("ctx", None),
        P("ctx", None),
        P("ctx", "head"),
        P("ctx", "head"),
        P("ctx", "head"),
        P(None, "head"),
        P(None, "head"),
        P(None, "head"),
    )
    return jax.shard_map(on_device, mesh=mesh, in_specs=in_specs, out_specs=P("ctx", "head"), check_vma=False)
```

profile of v0, /device:TPU:250, one launch (start us, length us, event | category | flops | bytes accessed | tf_op | source)
XLA Modules:
  0.0 402.0 jit_solution(2156960516569581471)
XLA Ops:
  0.0 3.2 shard_map.100
  3.3 0.8 collective-permute-start
  4.2 1.0 copy-done.2
  5.4 0.3 fusion
  5.7 3.5 collective-permute-done.got_ref
  9.3 0.3 collective-permute-start.1
  9.7 6.6 %collective-permute-done.1.more_ref = bf16[128,768]{1,0:T(8,128)(2,1)S(1)} collective-permute-done((bf16[128,768]{1,0:T(8,128)(2,1)S(1)}, bf16[128,768]{1,0:T(8,128)(2,1)S(1)}, u32[]{:S(2)}, u32[]{:S(2)}) %collective-permute-start.1) | collective-permute-done | bytes 196640 | tf_op jit(solution)/shard_map/ppermute | solution.py:40
  16.3 0.3 shard_map.103
  16.6 0.6 collective-permute-start.2
  17.2 2.4 collective-permute-start.4
  19.6 0.5 collective-permute-start.3
  20.2 0.7 shard_map.104
  20.9 3.0 collective-permute-done.3.refs_2_
  24.0 3.1 collective-permute-start.7
  27.4 4.1 %collective-permute-done.7.refs_0_.refs_1_ = bf16[128,512]{1,0:T(8,128)(2,1)S(1)} collective-permute-done((bf16[128,512]{1,0:T(8,128)(2,1)S(1)}, bf16[128,512]{1,0:T(8,128)(2,1)S(1)}, u32[]{:S(2)}, u32[]{:S(2)}) %collective-permute-start.7) | collective-permute-done | bytes 131104 | tf_op jit(solution)/shard_map/ppermute | solution.py:40
  31.5 23.4 %shard_map.106 = (f32[8,1024]{1,0:T(8,128)S(1)}, f32[8,1024]{1,0:T(8,128)S(1)}, f32[128,1024]{1,0:T(8,128)S(1)}) custom-call(s32[9]{0:T(128)S(1)} %get-tuple-element.252.base_ref, bf16[128,1024]{1,0:T(8,128)(2,1)S(1)} %get-tuple-element.141.refs_0_, bf16[512,256]{1,0:T(8,128)(2,1)S(1)} %shard_map.105.refs_1_.refs_2_, ...), custom_call_target="tpu_custom_call" | custom-call | flops 17179869184 | bytes 67108864 | tf_op jit(solution)/shard_map/pallas_call | solution.py:423
  54.8 1.9 shard_map.107
  56.9 1.5 collective-permute-start.12
  58.4 22.1 %collective-permute-start.13 = (bf16[1024,256]{1,0:T(8,128)(2,1)S(1)}, bf16[1024,256]{1,0:T(8,128)(2,1)S(1)}, u32[]{:S(2)}, u32[]{:S(2)}) collective-permute-start(bf16[1024,256]{1,0:T(8,128)(2,1)S(1)} %shard_map.109.refs_3_), channel_id=1, source_target_pairs={{0,4},{1,5},{2,6},{3,7},{4,0},{5,1},{6,2},{7,3},{8,12},{9,13},{10,... | collective-permute-start | bytes 1572872 | tf_op jit(solution)/shard_map/ppermute | solution.py:40
  80.5 44.9 %shard_map.111 = (f32[8,1024]{1,0:T(8,128)S(1)}, f32[8,1024]{1,0:T(8,128)S(1)}, f32[128,1024]{1,0:T(8,128)S(1)}, f32[8,1024]{1,0:T(8,128)S(1)}, f32[8,1024]{1,0:T(8,128)S(1)}, /*index=5*/f32[128,1024]{1,0:T(8,128)S(1)}) custom-call(s32[1]{0:T(128)} %bitcast.12.flag_ref, ...), custom_call_target="tpu_custom_call", output_to_operand_aliasing={{0}: (5, {}), {1}: (6, {}), {2}: (7, {}), {3}: (8, {}), {4}... | custom-call | flops 17179869184 | bytes 67108864 | tf_op jit(solution)/shard_map/pallas_call | solution.py:431
  125.5 45.3 %shard_map.113 = (f32[8,1024]{1,0:T(8,128)S(1)}, f32[8,1024]{1,0:T(8,128)S(1)}, f32[128,1024]{1,0:T(8,128)S(1)}, f32[8,1024]{1,0:T(8,128)S(1)}, f32[8,1024]{1,0:T(8,128)S(1)}, /*index=5*/f32[128,1024]{1,0:T(8,128)S(1)}) custom-call(s32[1]{0:T(128)} %bitcast.14.flag_ref, ...), custom_call_target="tpu_custom_call", output_to_operand_aliasing={{0}: (5, {}), {1}: (6, {}), {2}: (7, {}), {3}: (8, {}), {4}... | custom-call | flops 17179869184 | bytes 67108864 | tf_op jit(solution)/shard_map/pallas_call | solution.py:431
  171.0 2.1 shard_map.116
  173.1 1.0 collective-permute-start.14
  174.1 45.3 %shard_map.118 = (f32[8,1024]{1,0:T(8,128)S(1)}, f32[8,1024]{1,0:T(8,128)S(1)}, f32[128,1024]{1,0:T(8,128)S(1)}, f32[8,1024]{1,0:T(8,128)S(1)}, f32[8,1024]{1,0:T(8,128)S(1)}, /*index=5*/f32[128,1024]{1,0:T(8,128)S(1)}) custom-call(s32[1]{0:T(128)} %bitcast.16.flag_ref, ...), custom_call_target="tpu_custom_call", output_to_operand_aliasing={{0}: (5, {}), {1}: (6, {}), {2}: (7, {}), {3}: (8, {}), {4}... | custom-call | flops 17179869184 | bytes 67108864 | tf_op jit(solution)/shard_map/pallas_call | solution.py:431
  219.4 0.3 collective-permute-start.17
  219.7 44.0 %collective-permute-start.18 = (bf16[1024,256]{1,0:T(8,128)(2,1)S(1)}, bf16[1024,256]{1,0:T(8,128)(2,1)S(1)}, u32[]{:S(2)}, u32[]{:S(2)}) collective-permute-start(bf16[1024,256]{1,0:T(8,128)(2,1)S(1)} %shard_map.119.refs_3_), channel_id=1, source_target_pairs={{0,4},{1,5},{2,6},{3,7},{4,0},{5,1},{6,2},{7,3},{8,12},{9,13},{10,... | collective-permute-start | bytes 1572872 | tf_op jit(solution)/shard_map/ppermute | solution.py:40
  263.8 44.9 %shard_map.121 = (f32[8,1024]{1,0:T(8,128)S(1)}, f32[8,1024]{1,0:T(8,128)S(1)}, f32[128,1024]{1,0:T(8,128)S(1)}, f32[8,1024]{1,0:T(8,128)S(1)}, f32[8,1024]{1,0:T(8,128)S(1)}, /*index=5*/f32[128,1024]{1,0:T(8,128)S(1)}) custom-call(s32[1]{0:T(128)} %bitcast.15.flag_ref, ...), custom_call_target="tpu_custom_call", output_to_operand_aliasing={{0}: (5, {}), {1}: (6, {}), {2}: (7, {}), {3}: (8, {}), {4}... | custom-call | flops 17179869184 | bytes 67108864 | tf_op jit(solution)/shard_map/pallas_call | solution.py:431
  308.7 45.3 %shard_map.122 = (f32[8,1024]{1,0:T(8,128)S(1)}, f32[8,1024]{1,0:T(8,128)S(1)}, f32[128,1024]{1,0:T(8,128)S(1)}, f32[8,1024]{1,0:T(8,128)S(1)}, f32[8,1024]{1,0:T(8,128)S(1)}, /*index=5*/f32[128,1024]{1,0:T(8,128)S(1)}) custom-call(s32[1]{0:T(128)} %bitcast.17.flag_ref, ...), custom_call_target="tpu_custom_call", output_to_operand_aliasing={{0}: (5, {}), {1}: (6, {}), {2}: (7, {}), {3}: (8, {}), {4}... | custom-call | flops 17179869184 | bytes 67108864 | tf_op jit(solution)/shard_map/pallas_call | solution.py:431
  353.9 22.7 %shard_map.124 = bf16[128,1024]{1,0:T(8,128)(2,1)S(1)} custom-call(s32[1]{0:T(128)} %bitcast.flag_ref, bf16[128,512]{1,0:T(8,128)(2,1)S(1)} %collective-permute-done.7.refs_0_.refs_1_, bf16[128,512]{1,0:T(8,128)(2,1)S(1)} %collective-permute-done.8.refs_1_.refs_2_, bf16[512,256]{1,0:T(8,128)(2,1)S(1)} %collective-permute-done.14.refs_1_.refs_2_, ...), custom_call_target="tpu_custom_call" | custom-call | flops 17179869184 | bytes 67108864 | tf_op jit(solution)/shard_map/pallas_call | solution.py:462
  376.7 1.7 collective-permute-start.19
  378.4 22.7 %shard_map.123 = bf16[128,1024]{1,0:T(8,128)(2,1)S(1)} custom-call(s32[1]{0:T(128)} %bitcast.flag_ref, bf16[128,1024]{1,0:T(8,128)(2,1)S(1)} %get-tuple-element.141.refs_0_, bf16[512,256]{1,0:T(8,128)(2,1)S(1)} %collective-permute-done.14.refs_1_.refs_2_, bf16[512,256]{1,0:T(8,128)(2,1)S(1)} %collective-permute-done.17.refs_2_.refs_3_, ...), custom_call_target="tpu_custom_call" | custom-call | flops 17179869184 | bytes 67108864 | tf_op jit(solution)/shard_map/pallas_call | solution.py:462
  401.2 0.8 pad_maximum_fusion
  (64 shorter events, 1.5 us)
Async XLA Ops:
  0.0 4.2 %copy-start.7 = (s32[128,2]{0,1:T(2,128)S(1)}, s32[128,2]{0,1:T(2,128)}, u32[]{:S(2)}) copy-start(s32[128,2]{0,1:T(2,128)} %param.12) | copy-start | bytes 3076
  0.0 4.2 %copy-start.8 = (f32[128,2]{0,1:T(2,128)S(1)}, f32[128,2]{0,1:T(2,128)}, u32[]{:S(2)}) copy-start(f32[128,2]{0,1:T(2,128)} %param.13) | copy-start | bytes 3076
  3.3 6.0 %collective-permute-start = (bf16[128,768]{1,0:T(8,128)(2,1)}, bf16[128,768]{1,0:T(8,128)(2,1)S(1)}, u32[]{:S(2)}, u32[]{:S(2)}) collective-permute-start(bf16[128,768]{1,0:T(8,128)(2,1)} %get-tuple-element.126), channel_id=1, source_target_pairs={{0,1},{1,0},{2,3},{3,2},{4,7},{5,6},{6,5},{7,4},{8,9},{9,8},{10,11... | collective-permute-start | bytes 589832 | tf_op jit(solution)/shard_map/ppermute | solution.py:40
  4.2 1.0 copy-start.2
  9.2 7.0 %copy-start.3 = (bf16[256,256]{1,0:T(8,128)(2,1)S(1)}, bf16[256,256]{1,0:T(8,128)(2,1)}, u32[]{:S(2)}) copy-start(bf16[256,256]{1,0:T(8,128)(2,1)} %upk_ref.1) | copy-start | bytes 393220
  9.2 7.0 %copy-start.4 = (bf16[256,256]{1,0:T(8,128)(2,1)S(1)}, bf16[256,256]{1,0:T(8,128)(2,1)}, u32[]{:S(2)}) copy-start(bf16[256,256]{1,0:T(8,128)(2,1)} %upv_ref.1) | copy-start | bytes 393220
  9.2 7.0 %copy-start.5 = (bf16[128,256]{1,0:T(8,128)(2,1)S(1)}, bf16[128,256]{1,0:T(8,128)(2,1)}, u32[]{:S(2)}) copy-start(bf16[128,256]{1,0:T(8,128)(2,1)} %kb_ref.1) | copy-start | bytes 196612
  9.2 7.0 %copy-start.6 = (bf16[128,256]{1,0:T(8,128)(2,1)S(1)}, bf16[128,256]{1,0:T(8,128)(2,1)}, u32[]{:S(2)}) copy-start(bf16[128,256]{1,0:T(8,128)(2,1)} %vb_ref.1) | copy-start | bytes 196612
  9.3 7.0 %collective-permute-start.1 = (bf16[128,768]{1,0:T(8,128)(2,1)S(1)}, bf16[128,768]{1,0:T(8,128)(2,1)S(1)}, u32[]{:S(2)}, u32[]{:S(2)}) collective-permute-start(bf16[128,768]{1,0:T(8,128)(2,1)S(1)} %get-tuple-element.131), channel_id=1, source_target_pairs={{0,3},{1,2},{2,1},{3,0},{4,5},{5,4},{6,7},{7,6},{8,11},{9,10},{10,... | collective-permute-start | bytes 589832 | tf_op jit(solution)/shard_map/ppermute | solution.py:40
  16.3 3.9 copy-start
  16.3 3.9 copy-start.1
  16.6 4.4 %collective-permute-start.2 = (bf16[128,256]{1,0:T(8,128)(2,1)S(1)}, bf16[128,256]{1,0:T(8,128)(2,1)S(1)}, u32[]{:S(2)}, u32[]{:S(2)}) collective-permute-start(bf16[128,256]{1,0:T(8,128)(2,1)S(1)} %get-tuple-element.135), channel_id=1, source_target_pairs={{0,8},{1,9},{2,10},{3,11},{4,12},{5,13},{6,14},{7,15},{8,0},{9,1},... | collective-permute-start | bytes 196616 | tf_op jit(solution)/shard_map/ppermute | solution.py:40
  17.2 6.7 %collective-permute-start.4 = (bf16[128,256]{1,0:T(8,128)(2,1)S(1)}, bf16[128,256]{1,0:T(8,128)(2,1)S(1)}, u32[]{:S(2)}, u32[]{:S(2)}) collective-permute-start(bf16[128,256]{1,0:T(8,128)(2,1)S(1)} %get-tuple-element.135), channel_id=1, source_target_pairs={{0,16},{1,17},{2,18},{3,19},{4,20},{5,21},{6,22},{7,23},{8,24},{9,... | collective-permute-start | bytes 196616 | tf_op jit(solution)/shard_map/ppermute | solution.py:40
  19.6 4.3 %collective-permute-start.3 = (bf16[128,256]{1,0:T(8,128)(2,1)S(1)}, bf16[128,256]{1,0:T(8,128)(2,1)S(1)}, u32[]{:S(2)}, u32[]{:S(2)}) collective-permute-start(bf16[128,256]{1,0:T(8,128)(2,1)S(1)} %get-tuple-element.136.refs_0_), channel_id=1, source_target_pairs={{0,24},{1,25},{2,26},{3,27},{4,28},{5,29},{6,30},{7,31},{8,16},{9,... | collective-permute-start | bytes 196616 | tf_op jit(solution)/shard_map/ppermute | solution.py:40
  23.9 7.5 %collective-permute-start.6 = (bf16[512,256]{1,0:T(8,128)(2,1)S(1)}, bf16[512,256]{1,0:T(8,128)(2,1)S(1)}, u32[]{:S(2)}, u32[]{:S(2)}) collective-permute-start(bf16[512,256]{1,0:T(8,128)(2,1)S(1)} %shard_map.105.refs_1_.refs_2_), channel_id=1, source_target_pairs={{0,4},{1,5},{2,6},{3,7},{4,0},{5,1},{6,2},{7,3},{8,12},{9,13},{10,... | collective-permute-start | bytes 786440 | tf_op jit(solution)/shard_map/ppermute | solution.py:40
  24.0 7.4 %collective-permute-start.7 = (bf16[128,512]{1,0:T(8,128)(2,1)S(1)}, bf16[128,512]{1,0:T(8,128)(2,1)S(1)}, u32[]{:S(2)}, u32[]{:S(2)}) collective-permute-start(bf16[128,512]{1,0:T(8,128)(2,1)S(1)} %get-tuple-element.145), channel_id=1, source_target_pairs={{0,8},{1,9},{2,10},{3,11},{4,12},{5,13},{6,14},{7,15},{8,0},{9,1},... | collective-permute-start | bytes 393224 | tf_op jit(solution)/shard_map/ppermute | solution.py:40
  27.2 29.6 %collective-permute-start.5 = (bf16[512,256]{1,0:T(8,128)(2,1)S(1)}, bf16[512,256]{1,0:T(8,128)(2,1)S(1)}, u32[]{:S(2)}, u32[]{:S(2)}) collective-permute-start(bf16[512,256]{1,0:T(8,128)(2,1)S(1)} %shard_map.105.refs_1_.refs_2_), channel_id=1, source_target_pairs={{0,32},{1,33},{2,34},{3,35},{4,228},{5,229},{6,230},{7,231},{8,40}... | collective-permute-start | bytes 786440 | tf_op jit(solution)/shard_map/ppermute | solution.py:40
  27.2 27.6 %collective-permute-start.8 = (bf16[128,512]{1,0:T(8,128)(2,1)S(1)}, bf16[128,512]{1,0:T(8,128)(2,1)S(1)}, u32[]{:S(2)}, u32[]{:S(2)}) collective-permute-start(bf16[128,512]{1,0:T(8,128)(2,1)S(1)} %get-tuple-element.151), channel_id=1, source_target_pairs={{0,8},{1,9},{2,10},{3,11},{4,12},{5,13},{6,14},{7,15},{8,0},{9,1},... | collective-permute-start | bytes 393224 | tf_op jit(solution)/shard_map/ppermute | solution.py:40
  31.5 25.4 %collective-permute-start.10 = (bf16[512,256]{1,0:T(8,128)(2,1)S(1)}, bf16[512,256]{1,0:T(8,128)(2,1)S(1)}, u32[]{:S(2)}, u32[]{:S(2)}) collective-permute-start(bf16[512,256]{1,0:T(8,128)(2,1)S(1)} %collective-permute-done.6.refs_2_.refs_3_), channel_id=1, source_target_pairs={{0,32},{1,33},{2,34},{3,35},{4,228},{5,229},{6,230},{7,231},{8,40}... | collective-permute-start | bytes 786440 | tf_op jit(solution)/shard_map/ppermute | solution.py:40
  56.8 68.6 %collective-permute-start.9 = (bf16[512,256]{1,0:T(8,128)(2,1)S(1)}, bf16[512,256]{1,0:T(8,128)(2,1)S(1)}, u32[]{:S(2)}, u32[]{:S(2)}) collective-permute-start(bf16[512,256]{1,0:T(8,128)(2,1)S(1)} %collective-permute-done.5.seen_ref.refs_0_), channel_id=1, source_target_pairs={{0,32},{1,33},{2,34},{3,35},{4,228},{5,229},{6,230},{7,231},{8,40}... | collective-permute-start | bytes 786440 | tf_op jit(solution)/shard_map/ppermute | solution.py:40
  56.9 113.8 %collective-permute-start.12 = (bf16[512,256]{1,0:T(8,128)(2,1)S(1)}, bf16[512,256]{1,0:T(8,128)(2,1)S(1)}, u32[]{:S(2)}, u32[]{:S(2)}) collective-permute-start(bf16[512,256]{1,0:T(8,128)(2,1)S(1)} %collective-permute-done.10.refs_1_.seen_ref), channel_id=1, source_target_pairs={{0,32},{1,33},{2,34},{3,35},{4,228},{5,229},{6,230},{7,231},{8,40}... | collective-permute-start | bytes 786440 | tf_op jit(solution)/shard_map/ppermute | solution.py:40
  58.4 67.1 %collective-permute-start.13 = (bf16[1024,256]{1,0:T(8,128)(2,1)S(1)}, bf16[1024,256]{1,0:T(8,128)(2,1)S(1)}, u32[]{:S(2)}, u32[]{:S(2)}) collective-permute-start(bf16[1024,256]{1,0:T(8,128)(2,1)S(1)} %shard_map.109.refs_3_), channel_id=1, source_target_pairs={{0,4},{1,5},{2,6},{3,7},{4,0},{5,1},{6,2},{7,3},{8,12},{9,13},{10,... | collective-permute-start | bytes 1572872 | tf_op jit(solution)/shard_map/ppermute | solution.py:40
  125.4 47.7 %collective-permute-start.11 = (bf16[512,256]{1,0:T(8,128)(2,1)S(1)}, bf16[512,256]{1,0:T(8,128)(2,1)S(1)}, u32[]{:S(2)}, u32[]{:S(2)}) collective-permute-start(bf16[512,256]{1,0:T(8,128)(2,1)S(1)} %collective-permute-done.9.seen_ref.refs_0_), channel_id=1, source_target_pairs={{0,32},{1,33},{2,34},{3,35},{4,228},{5,229},{6,230},{7,231},{8,40}... | collective-permute-start | bytes 786440 | tf_op jit(solution)/shard_map/ppermute | solution.py:40
  170.8 48.6 %collective-permute-start.15 = (bf16[512,256]{1,0:T(8,128)(2,1)S(1)}, bf16[512,256]{1,0:T(8,128)(2,1)S(1)}, u32[]{:S(2)}, u32[]{:S(2)}) collective-permute-start(bf16[512,256]{1,0:T(8,128)(2,1)S(1)} %collective-permute-done.12.refs_1_.seen_ref), channel_id=1, source_target_pairs={{0,32},{1,33},{2,34},{3,35},{4,228},{5,229},{6,230},{7,231},{8,40}... | collective-permute-start | bytes 786440 | tf_op jit(solution)/shard_map/ppermute | solution.py:40
  170.9 3.2 collective-permute-start.16
  173.1 135.6 %collective-permute-start.14 = (bf16[512,256]{1,0:T(8,128)(2,1)S(1)}, bf16[512,256]{1,0:T(8,128)(2,1)S(1)}, u32[]{:S(2)}, u32[]{:S(2)}) collective-permute-start(bf16[512,256]{1,0:T(8,128)(2,1)S(1)} %collective-permute-done.11.seen_ref.refs_0_), channel_id=1, source_target_pairs={{0,32},{1,33},{2,34},{3,35},{4,228},{5,229},{6,230},{7,231},{8,40}... | collective-permute-start | bytes 786440 | tf_op jit(solution)/shard_map/ppermute | solution.py:40
  219.4 134.5 %collective-permute-start.17 = (bf16[512,256]{1,0:T(8,128)(2,1)S(1)}, bf16[512,256]{1,0:T(8,128)(2,1)S(1)}, u32[]{:S(2)}, u32[]{:S(2)}) collective-permute-start(bf16[512,256]{1,0:T(8,128)(2,1)S(1)} %collective-permute-done.15.refs_1_.seen_ref), channel_id=1, source_target_pairs={{0,32},{1,33},{2,34},{3,35},{4,228},{5,229},{6,230},{7,231},{8,40}... | collective-permute-start | bytes 786440 | tf_op jit(solution)/shard_map/ppermute | solution.py:40
  219.7 88.9 %collective-permute-start.18 = (bf16[1024,256]{1,0:T(8,128)(2,1)S(1)}, bf16[1024,256]{1,0:T(8,128)(2,1)S(1)}, u32[]{:S(2)}, u32[]{:S(2)}) collective-permute-start(bf16[1024,256]{1,0:T(8,128)(2,1)S(1)} %shard_map.119.refs_3_), channel_id=1, source_target_pairs={{0,4},{1,5},{2,6},{3,7},{4,0},{5,1},{6,2},{7,3},{8,12},{9,13},{10,... | collective-permute-start | bytes 1572872 | tf_op jit(solution)/shard_map/ppermute | solution.py:40
  376.7 24.4 %collective-permute-start.19 = (bf16[128,1024]{1,0:T(8,128)(2,1)S(1)}, bf16[128,1024]{1,0:T(8,128)(2,1)S(1)}, u32[]{:S(2)}, u32[]{:S(2)}) collective-permute-start(bf16[128,1024]{1,0:T(8,128)(2,1)S(1)} %shard_map.124), channel_id=1, source_target_pairs={{0,8},{1,9},{2,10},{3,11},{4,12},{5,13},{6,14},{7,15},{8,0},{9,1},... | collective-permute-start | bytes 786440 | tf_op jit(solution)/shard_map/ppermute | solution.py:40
where the time goes:
time: 402 us
  Pallas kernels  303 us (75%)
  starting transfers between devices  78.9 us (20%)
  waiting for transfers between devices  17.3 us (4%)
    pallas_call x6, Pallas kernels, attend(): call(kernel, 10, state_shape * 2, 1, aliases, spare + scratch)  228 us
    ppermute x20, starting transfers between devices, send(): return lax.ppermute(array, ('ctx', 'head'), pairs)  78.9 us
    pallas_call x2, Pallas kernels, finish(): call(last_kernel, len(query) + 5, (side_shape,), scratch=scratch)  45.5 us
    pallas_call x1, Pallas kernels, on_device(): call(functools.partial(first_kernel, 0), 3, state_shape, scratch=spare)  23.4 us
    ppermute x20, waiting for transfers between devices, send(): return lax.ppermute(array, ('ctx', 'head'), pairs)  17.3 us
  transfers between devices with their start and end apart: 20, of which 5 were waited for; matrix products, arithmetic and copies ran while one was open for 0% of the time, Pallas kernels for 69%

commit v1 on v0

--- a/solution.py
+++ b/solution.py
@@ -36,7 +36,9 @@
         for x in range(XS):
             for core in range(2):
                 for y in range(YS):
-                    pairs.append((device(z, x, core, y), device(*move(z, x, core, y))))
+                    target = move(z, x, core, y)
+                    if target is not None:
+                        pairs.append((device(z, x, core, y), device(*target)))
     return lax.ppermute(array, ("ctx", "head"), pairs)
 
 
@@ -235,7 +237,7 @@
 
 
 def next_kernel(flag_ref, *refs):
-    q_refs, kv_ref, ins, outs, spare, part_ref = refs[:3], refs[3], refs[4:10], refs[10:16], refs[16:18], refs[18]
+    q_refs, kv_ref, ins, outs, spare, part_ref = refs[:2], refs[2], refs[3:9], refs[9:15], refs[15:17], refs[17]
 
     @pl.when(flag_ref[0] == 0)
     def _():
@@ -262,44 +264,6 @@
             careful([q_refs[:1], q_refs[1:]], (kv_ref,), [outs[:3], outs[3:]], spare)
 
 
-def loop_kernel(flag_ref, *refs):
-    q_refs, kv_ref, ins, outs, spare = refs[:3], refs[3], refs[4:10], refs[10:16], refs[16:18]
-    sides_q, tops, totals, accs = refs[18:]
-
-    @pl.when(flag_ref[0] == 0)
-    def _():
-        for ref, given in zip(outs, ins):
-            ref[...] = given[...]
-
-    @pl.when(flag_ref[0] != 0)
-    def _():
-        sides_q[0] = q_refs[0][...]
-        sides_q[1, :, : SIDE // 2] = q_refs[1][...]
-        sides_q[1, :, SIDE // 2 :] = q_refs[2][...]
-        for side in range(2):
-            tops[side] = ins[3 * side][...]
-
-        def body(side, carry):
-            totals[side], accs[side], unused = part_of(queries([sides_q.at[side]]), kv_ref[...], tops[side])
-            return carry
-
-        lax.fori_loop(0, 2, body, 0)
-        room = jnp.max(totals[...]) <= ROOM
-
-        @pl.when(room)
-        def _():
-            for side in range(2):
-                outs[3 * side][...] = ins[3 * side][...]
-                outs[3 * side + 1][...] = ins[3 * side + 1][...] + totals[side]
-                outs[3 * side + 2][...] = ins[3 * side + 2][...] + accs[side]
-
-        @pl.when(jnp.logical_not(room))
-        def _():
-            for ref, given in zip(outs, ins):
-                ref[...] = given[...]
-            careful([q_refs[:1], q_refs[1:]], (kv_ref,), [outs[:3], outs[3:]], spare)
-
-
 def last_kernel(flag_ref, *refs):
     *q_refs, a_ref, b_ref, top_ref, total_ref, acc_ref, out_ref, spare_q, spare_kv, last_top, last_total, last_acc = refs
     last_total[...] = total_ref[...]
@@ -329,7 +293,7 @@
     return pl.BlockSpec(memory_space=pltpu.VMEM)
 
 
-def call(kernel, n_in, outs, n_scalar=1, aliases=None, scratch=()):
+def call(kernel, n_in, outs, n_scalar=1, aliases=None, scratch=(), flops=1 << 16):
     return pl.pallas_call(
         kernel,
         out_shape=outs,
@@ -338,12 +302,17 @@
         input_output_aliases=aliases or {},
         scratch_shapes=list(scratch),
         compiler_params=pltpu.CompilerParams(vmem_limit_bytes=VMEM_LIMIT),
-        cost_estimate=pl.CostEstimate(flops=1 << 34, bytes_accessed=1 << 26, transcendentals=0),
+        cost_estimate=pl.CostEstimate(flops=flops, bytes_accessed=flops >> 8, transcendentals=0),
     )
 
 
 def after(array, *others):
     return lax.optimization_barrier((array,) + others)
+
+
+def touch(seen, array, flops=1 << 34):
+    out = jax.ShapeDtypeStruct(array.shape, array.dtype)
+    return call(touch_kernel, 2, (out,), 0, {1: 0}, flops=flops)(seen, array)[0]
 
 
 def on_device(activations, adapter_down, adapter_ids, adapter_weight, query_base, key_base, value_base, up_query, up_key, up_value):
@@ -390,26 +359,34 @@
         send(kv_other, lambda z, x, c, y: (z, x ^ 2, c, y)),
     ]
     side_shape = shape((ROWS, GROUP * HD), b16)
-    piece_shape = shape((ROWS, GROUP * HD // 2), b16)
-    q_own, *q_other = call(q_kernel, 5, (side_shape, piece_shape, piece_shape))(
+    q_own, q_other = call(q_kernel, 5, (side_shape, side_shape))(
         groups, gated_query, up_query, query_base, cosine, sine
     )
-    *blocks_x, q_own, q_first, q_second = after(*blocks_x, q_own, *q_other)
+    q_rest = neighbour(q_other)
+    q_own = touch(q_other, q_own, 1 << 36)
+    *blocks_x, q_own = after(*blocks_x, q_own)
 
     def join(*parts):
         rows = sum(part.shape[0] for part in parts)
         return call(join_kernel, len(parts), (shape((rows, 2 * HD), b16),), 0)(*parts)[0]
 
     moving_a = join(kv, *blocks_x)
-    q_rest = [neighbour(q_first), neighbour(q_second)]
-
-    def ring(array):
-        return send(array, lambda z, x, c, y: (z + (1 if c == 0 else -1), x, c, y))
-
-    arriving_a = ring(moving_a)
+
+    def onward(step):
+        def move(z, x, core, y):
+            if core == 0:
+                return (z + 1, x, core, y) if step - 1 <= z < ZS - 1 else None
+            return (z - 1, x, core, y) if (z + step - 1) % ZS < ZS // 2 else None
+
+        return move
+
+    def ring(array, step):
+        return send(array, onward(step))
+
+    arriving_a = ring(moving_a, 1)
     moving_b = swap_cores(moving_a)
-    moving_b, q_rest[0] = after(moving_b, q_rest[0])
-    arriving_b = ring(moving_b)
+    arriving_b = ring(moving_b, 1)
+    q_own = touch(moving_b, q_own, 1 << 30)
 
     blocks = (jnp.stack([x, x ^ 1, x ^ 3, x ^ 2]) - x) * BLOCK
     keys_at = jnp.concatenate([blocks + core * ROWS, blocks + (1 - core) * ROWS])
@@ -422,49 +399,45 @@
     state = [
         *call(functools.partial(first_kernel, 0), 3, state_shape, scratch=spare)(bases(core * ROWS), q_own, moving_a, moving_b),
     ]
-    state += call(functools.partial(first_kernel, 1), 4, state_shape, scratch=spare)(
-        bases(((x ^ 1) - x) * BLOCK + core * ROWS), *q_rest, moving_a, moving_b
+    q_rest, *state = after(q_rest, *state)
+    state += call(functools.partial(first_kernel, 1), 3, state_shape, scratch=spare)(
+        bases(((x ^ 1) - x) * BLOCK + core * ROWS), q_rest, moving_a, moving_b
     )
 
-    def attend(kernel, scratch, flag, kv, state):
-        aliases = {5 + k: k for k in range(6)}
-        return call(kernel, 10, state_shape * 2, 1, aliases, spare + scratch)(
-            flag.astype(jnp.int32).reshape(1), q_own, *q_rest, kv, *state
+    def attend(flag, kv, state):
+        aliases = {4 + k: k for k in range(6)}
+        scratch = [*spare, pltpu.VMEM((HD, 2 * SIDE), f32)]
+        return call(next_kernel, 9, state_shape * 2, 1, aliases, scratch)(
+            flag.astype(jnp.int32).reshape(1), q_own, q_rest, kv, *state
         )
 
-    near = functools.partial(attend, next_kernel, [pltpu.VMEM((HD, 2 * SIDE), f32)])
-    sides = [((2, ROWS, SIDE), b16), ((2, 8, SIDE), f32), ((2, 8, SIDE), f32), ((2, HD, SIDE), f32)]
-    away = functools.partial(attend, loop_kernel, [pltpu.VMEM(*side) for side in sides])
-
-    def take(arriving, state, on):
+    def take(arriving, state, step, flops=1 << 34):
         arrived, *state = after(arriving, *state)
-        if not on:
+        if step > 4:
             return arrived, None, state
-        arriving = ring(arrived)
-        top = call(touch_kernel, 2, state_shape[:1], 0, {1: 0})(arrived, state[0])[0]
-        return arrived, arriving, [top, *state[1:]]
-
-    next_a, arriving_a, state = take(arriving_a, state, True)
+        arriving = ring(arrived, step)
+        return arrived, arriving, [touch(arrived, state[0], flops), *state[1:]]
+
+    moving_a, arriving_a, state = take(arriving_a, state, 2, 1 << 31)
     for step in range(1, 4):
         below, wrapped = z >= step, z + step >= ZS
-        moving_b, arriving_b, state = take(arriving_b, state, True)
-        moving = join(next_a, moving_b)
+        moving_b, arriving_b, state = take(arriving_b, state, step + 1)
+        moving = join(moving_a, moving_b)
         swapped = swap_cores(moving)
-        state = near(jnp.where(core == 0, below, wrapped), moving, state)
-        next_a, arriving_a, state = take(arriving_a, state, step < 3)
-        state = away(jnp.where(core == 0, wrapped, below), swapped, state)
-    moving_a = next_a
+        state = attend(jnp.where(core == 0, below, wrapped), moving, state)
+        moving_a, arriving_a, state = take(arriving_a, state, step + 2)
+        state = attend(jnp.where(core == 0, wrapped, below), swapped, state)
     moving_b, *state = after(arriving_b, *state)
     flag = (z >= ZS // 2).astype(jnp.int32).reshape(1)
 
     def finish(query, state):
         scratch = spare + [pltpu.VMEM((8, SIDE), f32)] * 2 + [pltpu.VMEM((HD, SIDE), f32)]
-        return call(last_kernel, len(query) + 5, (side_shape,), scratch=scratch)(
-            flag, *query, moving_a, moving_b, *state
+        return call(last_kernel, 6, (side_shape,), scratch=scratch)(
+            flag, query, moving_a, moving_b, *state
         )[0]
 
     back = neighbour(finish(q_rest, state[3:]))
-    own = finish([q_own], state[:3])
+    own = finish(q_own, state[:3])
     return jnp.concatenate([jnp.where(group == 0, own, back), jnp.where(group == 0, back, own)], axis=1)
 
 

time: 402 us -> 408 us (1.015)
  the two profiles are of different devices: /device:TPU:250 before, /device:TPU:161 now
where the time goes in v1:
time: 408 us
  Pallas kernels  277 us (68%)
  starting transfers between devices  118 us (29%)
  waiting for transfers between devices  9.68 us (2%)
    pallas_call x6, Pallas kernels, attend(): call(next_kernel, 9, state_shape * 2, 1, aliases, scratch)  180 us
    ppermute x19, starting transfers between devices, send(): return lax.ppermute(array, ('ctx', 'head'), pairs)  118 us
    pallas_call x2, Pallas kernels, finish(): call(last_kernel, 6, (side_shape,), scratch=scratch)  45.5 us
    pallas_call x1, Pallas kernels, on_device(): call(functools.partial(first_kernel, 1), 3, state_shape, scratch=spare)  23.4 us
    pallas_call x1, Pallas kernels, on_device(): call(functools.partial(first_kernel, 0), 3, state_shape, scratch=spare)  23.4 us
    ppermute x19, waiting for transfers between devices, send(): return lax.ppermute(array, ('ctx', 'head'), pairs)  9.68 us
  transfers between devices with their start and end apart: 19, of which 5 were waited for; matrix products, arithmetic and copies ran while one was open for 0% of the time, Pallas kernels for 61%

profile of v1, /device:TPU:161, one launch (start us, length us, event | category | flops | bytes accessed | tf_op | source)
XLA Modules:
  0.0 407.9 jit_solution(1593120190848764662)
XLA Ops:
  0.1 3.3 shard_map.100
  3.4 2.8 collective-permute-start
  6.4 1.0 copy-done.2
  7.8 1.7 collective-permute-done.got_ref
  9.6 0.4 collective-permute-start.1
  10.0 4.1 %collective-permute-done.1.more_ref = bf16[128,768]{1,0:T(8,128)(2,1)S(1)} collective-permute-done((bf16[128,768]{1,0:T(8,128)(2,1)S(1)}, bf16[128,768]{1,0:T(8,128)(2,1)S(1)}, u32[]{:S(2)}, u32[]{:S(2)}) %collective-permute-start.1) | collective-permute-done | bytes 196640 | tf_op jit(solution)/shard_map/ppermute | solution.py:42
  14.5 1.3 collective-permute-start.2
  15.8 2.5 collective-permute-start.4
  18.4 0.7 shard_map.104
  19.2 3.3 collective-permute-done.3.refs_2_
  22.6 4.7 %collective-permute-start.5 = (bf16[512,256]{1,0:T(8,128)(2,1)S(1)}, bf16[512,256]{1,0:T(8,128)(2,1)S(1)}, u32[]{:S(2)}, u32[]{:S(2)}) collective-permute-start(bf16[512,256]{1,0:T(8,128)(2,1)S(1)} %shard_map.106.refs_1_), channel_id=1, source_target_pairs={{0,4},{1,5},{2,6},{3,7},{4,0},{5,1},{6,2},{7,3},{8,12},{9,13},{10,... | collective-permute-start | bytes 786440 | tf_op jit(solution)/shard_map/ppermute | solution.py:42
  27.3 0.7 collective-permute-start.6
  28.1 0.3 collective-permute-done.5.seen_ref.refs_2_
  28.4 0.7 collective-permute-start.9
  29.1 23.4 %shard_map.108 = (f32[8,1024]{1,0:T(8,128)S(1)}, f32[8,1024]{1,0:T(8,128)S(1)}, f32[128,1024]{1,0:T(8,128)S(1)}) custom-call(s32[9]{0:T(128)S(1)} %get-tuple-element.250.base_ref, bf16[128,1024]{1,0:T(8,128)(2,1)S(1)} %shard_map.107.refs_0_, bf16[512,256]{1,0:T(8,128)(2,1)S(1)} %shard_map.106.refs_1_, ...), custom_call_target="tpu_custom_call" | custom-call | flops 65536 | bytes 256 | tf_op jit(solution)/shard_map/pallas_call | solution.py:400
  52.5 23.4 %shard_map.109 = (f32[8,1024]{1,0:T(8,128)S(1)}, f32[8,1024]{1,0:T(8,128)S(1)}, f32[128,1024]{1,0:T(8,128)S(1)}) custom-call(s32[9]{0:T(128)S(1)} %get-tuple-element.249.base_ref, bf16[128,1024]{1,0:T(8,128)(2,1)S(1)} %collective-permute-done.7.refs_0_.refs_1_, bf16[512,256]{1,0:T(8,128)(2,1)S(1)} %shard_map.106.refs_1_, ...), custom_call_target="tpu_custom_call" | custom-call | flops 65536 | bytes 256 | tf_op jit(solution)/shard_map/pallas_call | solution.py:403
  76.0 0.7 collective-permute-start.8
  76.7 0.7 collective-permute-start.11
  77.5 0.3 shard_map.113
  77.9 1.3 collective-permute-start.10
  79.4 44.9 %shard_map.115 = (f32[8,1024]{1,0:T(8,128)S(1)}, f32[8,1024]{1,0:T(8,128)S(1)}, f32[128,1024]{1,0:T(8,128)S(1)}, f32[8,1024]{1,0:T(8,128)S(1)}, f32[8,1024]{1,0:T(8,128)S(1)}, /*index=5*/f32[128,1024]{1,0:T(8,128)S(1)}) custom-call(s32[1]{0:T(128)} %bitcast.14.flag_ref, ...), custom_call_target="tpu_custom_call", output_to_operand_aliasing={{0}: (4, {}), {1}: (5, {}), {2}: (6, {}), {3}: (7, {}), {4}... | custom-call | flops 65536 | bytes 256 | tf_op jit(solution)/shard_map/pallas_call | solution.py:410
  124.3 1.3 collective-permute-start.14
  125.7 7.0 %collective-permute-start.15 = (bf16[1024,256]{1,0:T(8,128)(2,1)S(1)}, bf16[1024,256]{1,0:T(8,128)(2,1)S(1)}, u32[]{:S(2)}, u32[]{:S(2)}) collective-permute-start(bf16[1024,256]{1,0:T(8,128)(2,1)S(1)} %shard_map.116.refs_2_), channel_id=1, source_target_pairs={{0,4},{1,5},{2,6},{3,7},{4,0},{5,1},{6,2},{7,3},{8,12},{9,13},{10,... | collective-permute-start | bytes 1572872 | tf_op jit(solution)/shard_map/ppermute | solution.py:42
  132.9 1.9 collective-permute-start.13
  134.8 44.9 %shard_map.120 = (f32[8,1024]{1,0:T(8,128)S(1)}, f32[8,1024]{1,0:T(8,128)S(1)}, f32[128,1024]{1,0:T(8,128)S(1)}, f32[8,1024]{1,0:T(8,128)S(1)}, f32[8,1024]{1,0:T(8,128)S(1)}, /*index=5*/f32[128,1024]{1,0:T(8,128)S(1)}) custom-call(s32[1]{0:T(128)} %bitcast.16.flag_ref, ...), custom_call_target="tpu_custom_call", output_to_operand_aliasing={{0}: (4, {}), {1}: (5, {}), {2}: (6, {}), {3}: (7, {}), {4}... | custom-call | flops 65536 | bytes 256 | tf_op jit(solution)/shard_map/pallas_call | solution.py:410
  179.8 1.9 collective-permute-start.16
  181.7 89.6 %collective-permute-start.17 = (bf16[1024,256]{1,0:T(8,128)(2,1)S(1)}, bf16[1024,256]{1,0:T(8,128)(2,1)S(1)}, u32[]{:S(2)}, u32[]{:S(2)}) collective-permute-start(bf16[1024,256]{1,0:T(8,128)(2,1)S(1)} %shard_map.121.refs_2_), channel_id=1, source_target_pairs={{0,4},{1,5},{2,6},{3,7},{4,0},{5,1},{6,2},{7,3},{8,12},{9,13},{10,... | collective-permute-start | bytes 1572872 | tf_op jit(solution)/shard_map/ppermute | solution.py:42
  271.3 44.9 %shard_map.123 = (f32[8,1024]{1,0:T(8,128)S(1)}, f32[8,1024]{1,0:T(8,128)S(1)}, f32[128,1024]{1,0:T(8,128)S(1)}, f32[8,1024]{1,0:T(8,128)S(1)}, f32[8,1024]{1,0:T(8,128)S(1)}, /*index=5*/f32[128,1024]{1,0:T(8,128)S(1)}) custom-call(s32[1]{0:T(128)} %bitcast.15.flag_ref, ...), custom_call_target="tpu_custom_call", output_to_operand_aliasing={{0}: (4, {}), {1}: (5, {}), {2}: (6, {}), {3}: (7, {}), {4}... | custom-call | flops 65536 | bytes 256 | tf_op jit(solution)/shard_map/pallas_call | solution.py:410
  316.2 45.1 %shard_map.124 = (f32[8,1024]{1,0:T(8,128)S(1)}, f32[8,1024]{1,0:T(8,128)S(1)}, f32[128,1024]{1,0:T(8,128)S(1)}, f32[8,1024]{1,0:T(8,128)S(1)}, f32[8,1024]{1,0:T(8,128)S(1)}, /*index=5*/f32[128,1024]{1,0:T(8,128)S(1)}) custom-call(s32[1]{0:T(128)} %bitcast.17.flag_ref, ...), custom_call_target="tpu_custom_call", output_to_operand_aliasing={{0}: (4, {}), {1}: (5, {}), {2}: (6, {}), {3}: (7, {}), {4}... | custom-call | flops 65536 | bytes 256 | tf_op jit(solution)/shard_map/pallas_call | solution.py:410
  361.4 22.8 %shard_map.126 = bf16[128,1024]{1,0:T(8,128)(2,1)S(1)} custom-call(s32[1]{0:T(128)} %bitcast.flag_ref, bf16[128,1024]{1,0:T(8,128)(2,1)S(1)} %collective-permute-done.7.refs_0_.refs_1_, bf16[512,256]{1,0:T(8,128)(2,1)S(1)} %collective-permute-done.13.refs_1_, bf16[512,256]{1,0:T(8,128)(2,1)S(1)} %collective-permute-done.16.refs_2_, ...), custom_call_target="tpu_custom_call" | custom-call | flops 65536 | bytes 256 | tf_op jit(solution)/shard_map/pallas_call | solution.py:435
  384.2 22.7 %shard_map.125 = bf16[128,1024]{1,0:T(8,128)(2,1)S(1)} custom-call(s32[1]{0:T(128)} %bitcast.flag_ref, bf16[128,1024]{1,0:T(8,128)(2,1)S(1)} %shard_map.107.refs_0_, bf16[512,256]{1,0:T(8,128)(2,1)S(1)} %collective-permute-done.13.refs_1_, bf16[512,256]{1,0:T(8,128)(2,1)S(1)} %collective-permute-done.16.refs_2_, f32[8,1024]{1,0:T(8,128)S(1)} %get-tuple-element.239.refs_3_, ...), custom_call_target="tpu_custom_call" | custom-call | flops 65536 | bytes 256 | tf_op jit(solution)/shard_map/pallas_call | solution.py:435
  407.0 0.8 pad_maximum_fusion
  (64 shorter events, 2.2 us)
Async XLA Ops:
  0.0 6.3 %copy-start.7 = (s32[128,2]{0,1:T(2,128)S(1)}, s32[128,2]{0,1:T(2,128)}, u32[]{:S(2)}) copy-start(s32[128,2]{0,1:T(2,128)} %param.12) | copy-start | bytes 3076
  0.0 6.3 %copy-start.8 = (f32[128,2]{0,1:T(2,128)S(1)}, f32[128,2]{0,1:T(2,128)}, u32[]{:S(2)}) copy-start(f32[128,2]{0,1:T(2,128)} %param.13) | copy-start | bytes 3076
  0.0 14.2 %copy-start.5 = (bf16[128,256]{1,0:T(8,128)(2,1)S(1)}, bf16[128,256]{1,0:T(8,128)(2,1)}, u32[]{:S(2)}) copy-start(bf16[128,256]{1,0:T(8,128)(2,1)} %kb_ref.1) | copy-start | bytes 196612
  0.0 14.2 %copy-start.6 = (bf16[128,256]{1,0:T(8,128)(2,1)S(1)}, bf16[128,256]{1,0:T(8,128)(2,1)}, u32[]{:S(2)}) copy-start(bf16[128,256]{1,0:T(8,128)(2,1)} %vb_ref.1) | copy-start | bytes 196612
  0.0 14.2 %copy-start.3 = (bf16[256,256]{1,0:T(8,128)(2,1)S(1)}, bf16[256,256]{1,0:T(8,128)(2,1)}, u32[]{:S(2)}) copy-start(bf16[256,256]{1,0:T(8,128)(2,1)} %upk_ref.1) | copy-start | bytes 393220
  0.0 14.2 %copy-start.4 = (bf16[256,256]{1,0:T(8,128)(2,1)S(1)}, bf16[256,256]{1,0:T(8,128)(2,1)}, u32[]{:S(2)}) copy-start(bf16[256,256]{1,0:T(8,128)(2,1)} %upv_ref.1) | copy-start | bytes 393220
  0.0 18.4 %copy-start.1 = (bf16[128,2048]{1,0:T(8,128)(2,1)S(1)}, bf16[128,2048]{1,0:T(8,128)(2,1)}, u32[]{:S(2)}) copy-start(bf16[128,2048]{1,0:T(8,128)(2,1)} %qb_ref.1) | copy-start | bytes 1572868
  0.0 18.4 %copy-start = (bf16[256,2048]{1,0:T(8,128)(2,1)S(1)}, bf16[256,2048]{1,0:T(8,128)(2,1)}, u32[]{:S(2)}) copy-start(bf16[256,2048]{1,0:T(8,128)(2,1)} %upq_ref.1) | copy-start | bytes 3145732
  3.4 6.1 %collective-permute-start = (bf16[128,768]{1,0:T(8,128)(2,1)}, bf16[128,768]{1,0:T(8,128)(2,1)S(1)}, u32[]{:S(2)}, u32[]{:S(2)}) collective-permute-start(bf16[128,768]{1,0:T(8,128)(2,1)} %get-tuple-element.125), channel_id=1, source_target_pairs={{0,1},{1,0},{2,3},{3,2},{4,7},{5,6},{6,5},{7,4},{8,9},{9,8},{10,11... | collective-permute-start | bytes 589832 | tf_op jit(solution)/shard_map/ppermute | solution.py:42
  6.4 1.0 copy-start.2
  9.6 4.6 %collective-permute-start.1 = (bf16[128,768]{1,0:T(8,128)(2,1)S(1)}, bf16[128,768]{1,0:T(8,128)(2,1)S(1)}, u32[]{:S(2)}, u32[]{:S(2)}) collective-permute-start(bf16[128,768]{1,0:T(8,128)(2,1)S(1)} %get-tuple-element.130), channel_id=1, source_target_pairs={{0,3},{1,2},{2,1},{3,0},{4,5},{5,4},{6,7},{7,6},{8,11},{9,10},{10,... | collective-permute-start | bytes 589832 | tf_op jit(solution)/shard_map/ppermute | solution.py:42
  14.5 4.8 %collective-permute-start.2 = (bf16[128,256]{1,0:T(8,128)(2,1)S(1)}, bf16[128,256]{1,0:T(8,128)(2,1)S(1)}, u32[]{:S(2)}, u32[]{:S(2)}) collective-permute-start(bf16[128,256]{1,0:T(8,128)(2,1)S(1)} %get-tuple-element.135), channel_id=1, source_target_pairs={{0,8},{1,9},{2,10},{3,11},{4,12},{5,13},{6,14},{7,15},{8,0},{9,1},... | collective-permute-start | bytes 196616 | tf_op jit(solution)/shard_map/ppermute | solution.py:42
  15.8 6.8 %collective-permute-start.4 = (bf16[128,256]{1,0:T(8,128)(2,1)S(1)}, bf16[128,256]{1,0:T(8,128)(2,1)S(1)}, u32[]{:S(2)}, u32[]{:S(2)}) collective-permute-start(bf16[128,256]{1,0:T(8,128)(2,1)S(1)} %get-tuple-element.135), channel_id=1, source_target_pairs={{0,16},{1,17},{2,18},{3,19},{4,20},{5,21},{6,22},{7,23},{8,24},{9,... | collective-permute-start | bytes 196616 | tf_op jit(solution)/shard_map/ppermute | solution.py:42
  18.2 4.3 %collective-permute-start.3 = (bf16[128,256]{1,0:T(8,128)(2,1)S(1)}, bf16[128,256]{1,0:T(8,128)(2,1)S(1)}, u32[]{:S(2)}, u32[]{:S(2)}) collective-permute-start(bf16[128,256]{1,0:T(8,128)(2,1)S(1)} %get-tuple-element.134.refs_0_), channel_id=1, source_target_pairs={{0,24},{1,25},{2,26},{3,27},{4,28},{5,29},{6,30},{7,31},{8,16},{9,... | collective-permute-start | bytes 196616 | tf_op jit(solution)/shard_map/ppermute | solution.py:42
  19.1 33.4 %collective-permute-start.7 = (bf16[128,1024]{1,0:T(8,128)(2,1)S(1)}, bf16[128,1024]{1,0:T(8,128)(2,1)S(1)}, u32[]{:S(2)}, u32[]{:S(2)}) collective-permute-start(bf16[128,1024]{1,0:T(8,128)(2,1)S(1)} %get-tuple-element.137.seen_ref), channel_id=1, source_target_pairs={{0,8},{1,9},{2,10},{3,11},{4,12},{5,13},{6,14},{7,15},{8,0},{9,1},... | collective-permute-start | bytes 786440 | tf_op jit(solution)/shard_map/ppermute | solution.py:42
  22.6 5.9 %collective-permute-start.5 = (bf16[512,256]{1,0:T(8,128)(2,1)S(1)}, bf16[512,256]{1,0:T(8,128)(2,1)S(1)}, u32[]{:S(2)}, u32[]{:S(2)}) collective-permute-start(bf16[512,256]{1,0:T(8,128)(2,1)S(1)} %shard_map.106.refs_1_), channel_id=1, source_target_pairs={{0,4},{1,5},{2,6},{3,7},{4,0},{5,1},{6,2},{7,3},{8,12},{9,13},{10,... | collective-permute-start | bytes 786440 | tf_op jit(solution)/shard_map/ppermute | solution.py:42
  27.3 48.7 %collective-permute-start.6 = (bf16[512,256]{1,0:T(8,128)(2,1)S(1)}, bf16[512,256]{1,0:T(8,128)(2,1)S(1)}, u32[]{:S(2)}, u32[]{:S(2)}) collective-permute-start(bf16[512,256]{1,0:T(8,128)(2,1)S(1)} %shard_map.106.refs_1_), channel_id=1, source_target_pairs={{0,32},{1,33},{2,34},{3,35},{4,228},{5,229},{6,230},{7,231},{8,40}... | collective-permute-start | bytes 786440 | tf_op jit(solution)/shard_map/ppermute | solution.py:42
  28.4 48.3 %collective-permute-start.9 = (bf16[512,256]{1,0:T(8,128)(2,1)S(1)}, bf16[512,256]{1,0:T(8,128)(2,1)S(1)}, u32[]{:S(2)}, u32[]{:S(2)}) collective-permute-start(bf16[512,256]{1,0:T(8,128)(2,1)S(1)} %collective-permute-done.5.seen_ref.refs_2_), channel_id=1, source_target_pairs={{0,32},{1,33},{2,34},{3,35},{4,228},{5,229},{6,230},{7,231},{8,40}... | collective-permute-start | bytes 786440 | tf_op jit(solution)/shard_map/ppermute | solution.py:42
  76.0 1.9 collective-permute-start.8
  76.7 47.6 %collective-permute-start.11 = (bf16[512,256]{1,0:T(8,128)(2,1)S(1)}, bf16[512,256]{1,0:T(8,128)(2,1)S(1)}, u32[]{:S(2)}, u32[]{:S(2)}) collective-permute-start(bf16[512,256]{1,0:T(8,128)(2,1)S(1)} %collective-permute-done.9.refs_1_.seen_ref), channel_id=1, source_target_pairs={{4,228},{5,229},{6,230},{7,231},{12,236},{13,237},{14,238},{15,239... | collective-permute-start | bytes 786440 | tf_op jit(solution)/shard_map/ppermute | solution.py:42
  77.4 2.0 collective-permute-start.12
  77.9 55.0 %collective-permute-start.10 = (bf16[512,256]{1,0:T(8,128)(2,1)S(1)}, bf16[512,256]{1,0:T(8,128)(2,1)S(1)}, u32[]{:S(2)}, u32[]{:S(2)}) collective-permute-start(bf16[512,256]{1,0:T(8,128)(2,1)S(1)} %collective-permute-done.8.seen_ref.refs_0_), channel_id=1, source_target_pairs={{4,228},{5,229},{6,230},{7,231},{12,236},{13,237},{14,238},{15,239... | collective-permute-start | bytes 786440 | tf_op jit(solution)/shard_map/ppermute | solution.py:42
  124.3 55.4 %collective-permute-start.14 = (bf16[512,256]{1,0:T(8,128)(2,1)S(1)}, bf16[512,256]{1,0:T(8,128)(2,1)S(1)}, u32[]{:S(2)}, u32[]{:S(2)}) collective-permute-start(bf16[512,256]{1,0:T(8,128)(2,1)S(1)} %collective-permute-done.11.refs_1_.seen_ref), channel_id=1, source_target_pairs={{4,228},{5,229},{6,230},{7,231},{12,236},{13,237},{14,238},{15,239... | collective-permute-start | bytes 786440 | tf_op jit(solution)/shard_map/ppermute | solution.py:42
  125.7 9.1 %collective-permute-start.15 = (bf16[1024,256]{1,0:T(8,128)(2,1)S(1)}, bf16[1024,256]{1,0:T(8,128)(2,1)S(1)}, u32[]{:S(2)}, u32[]{:S(2)}) collective-permute-start(bf16[1024,256]{1,0:T(8,128)(2,1)S(1)} %shard_map.116.refs_2_), channel_id=1, source_target_pairs={{0,4},{1,5},{2,6},{3,7},{4,0},{5,1},{6,2},{7,3},{8,12},{9,13},{10,... | collective-permute-start | bytes 1572872 | tf_op jit(solution)/shard_map/ppermute | solution.py:42
  132.9 183.3 %collective-permute-start.13 = (bf16[512,256]{1,0:T(8,128)(2,1)S(1)}, bf16[512,256]{1,0:T(8,128)(2,1)S(1)}, u32[]{:S(2)}, u32[]{:S(2)}) collective-permute-start(bf16[512,256]{1,0:T(8,128)(2,1)S(1)} %collective-permute-done.10.seen_ref.refs_0_), channel_id=1, source_target_pairs={{4,228},{5,229},{6,230},{7,231},{12,236},{13,237},{14,238},{15,239... | collective-permute-start | bytes 786440 | tf_op jit(solution)/shard_map/ppermute | solution.py:42
  179.8 181.6 %collective-permute-start.16 = (bf16[512,256]{1,0:T(8,128)(2,1)S(1)}, bf16[512,256]{1,0:T(8,128)(2,1)S(1)}, u32[]{:S(2)}, u32[]{:S(2)}) collective-permute-start(bf16[512,256]{1,0:T(8,128)(2,1)S(1)} %collective-permute-done.14.refs_1_.seen_ref), channel_id=1, source_target_pairs={{4,228},{5,229},{6,230},{7,231},{12,236},{13,237},{14,238},{15,239... | collective-permute-start | bytes 786440 | tf_op jit(solution)/shard_map/ppermute | solution.py:42
  181.7 134.5 %collective-permute-start.17 = (bf16[1024,256]{1,0:T(8,128)(2,1)S(1)}, bf16[1024,256]{1,0:T(8,128)(2,1)S(1)}, u32[]{:S(2)}, u32[]{:S(2)}) collective-permute-start(bf16[1024,256]{1,0:T(8,128)(2,1)S(1)} %shard_map.121.refs_2_), channel_id=1, source_target_pairs={{0,4},{1,5},{2,6},{3,7},{4,0},{5,1},{6,2},{7,3},{8,12},{9,13},{10,... | collective-permute-start | bytes 1572872 | tf_op jit(solution)/shard_map/ppermute | solution.py:42
  384.1 22.9 %collective-permute-start.18 = (bf16[128,1024]{1,0:T(8,128)(2,1)S(1)}, bf16[128,1024]{1,0:T(8,128)(2,1)S(1)}, u32[]{:S(2)}, u32[]{:S(2)}) collective-permute-start(bf16[128,1024]{1,0:T(8,128)(2,1)S(1)} %shard_map.126), channel_id=1, source_target_pairs={{0,8},{1,9},{2,10},{3,11},{4,12},{5,13},{6,14},{7,15},{8,0},{9,1},... | collective-permute-start | bytes 786440 | tf_op jit(solution)/shard_map/ppermute | solution.py:42
